TPU v7x, 32 devices: a whole 2x2x4 slice. The times are simulated.
32 devices in a mesh: groups: 2 (over x), resp: 16 (over z, y, core).
Axes of the slice: x: 2, y: 2, z: 4, core: 2. Of those that a mesh axis runs over, the one named last changes fastest.
Arguments:
- queries: bfloat16 [32, 128, 2048], P(('groups', 'resp')), parts along dimension 0, may hold values from -6 to 6
- resp_keys: bfloat16 [32, 128, 512], P(('groups', 'resp')), parts along dimension 0, may hold values from -6 to 6
- resp_values: bfloat16 [32, 128, 512], P(('groups', 'resp')), parts along dimension 0, may hold values from -6 to 6
- out_grad: bfloat16 [32, 128, 2048], P(('groups', 'resp')), parts along dimension 0, may hold values from -6 to 6
- resp_lengths: int32 [32], P(('groups', 'resp')), parts along dimension 0, may hold values from 1 to 128, 1280 in all
- prompt_keys: bfloat16 [1024, 512], P(('groups', 'resp')), parts along dimension 0, may hold values from -6 to 6
- prompt_values: bfloat16 [1024, 512], P(('groups', 'resp')), parts along dimension 0, may hold values from -6 to 6
- prompt_length: int32 [2], P('groups'), parts along dimension 0, may hold values from 256 to 512
Outputs:
- attn_out: bfloat16 [32, 128, 2048], P(('groups', 'resp')), parts along dimension 0
- query_grad: bfloat16 [32, 128, 2048], P(('groups', 'resp')), parts along dimension 0
- key_grad: bfloat16 [32, 128, 512], P(('groups', 'resp')), parts along dimension 0
- value_grad: bfloat16 [32, 128, 512], P(('groups', 'resp')), parts along dimension 0
- prompt_key_grad: float32 [1024, 512], P(('groups', 'resp')), parts along dimension 0
- prompt_value_grad: float32 [1024, 512], P(('groups', 'resp')), parts along dimension 0
There are 2 independent parts, one for each index of `groups`. A program takes and returns all parts, laid end to end along the dimension named above; each array names one. Nothing has to cross between parts.
All inputs are finite; a program needn't handle non-finite values. No bound on the sum of `resp_lengths` on one device may be relied on, other than what follows from the above.
Results may differ from a plain program's by a relative error of at most 0.0095.
Values may be sent and summed in bfloat16 or wider, within the bound.
A program may use at most 64 MiB of HBM per device.

v0:
```python
import jax
import jax.numpy as jnp
from jax import lax
from jax.sharding import PartitionSpec as P

HEADS = 16
KV_HEADS = 4
HEAD_DIM = 128


def product(form, left, right):
    return jnp.einsum(form, left, right, preferred_element_type=jnp.float32)


def head_core(
    query_head,
    key_self,
    value_self,
    grad_head,
    key_prompt,
    value_prompt,
    live_prompt,
    causal,
    row_mask,
):
    scaling = query_head.shape[-1] ** (-0.5)
    prompt_rows = key_prompt.shape[0]
    score_prompt = product("rigd,pd->rgip", query_head, key_prompt) * scaling
    score_prompt = jnp.where(live_prompt[None, None, None, :], score_prompt, -jnp.inf)
    score_self = product("rigd,rjd->rgij", query_head, key_self) * scaling
    score_self = jnp.where(causal[None, None], score_self, -jnp.inf)
    scores = jnp.concatenate([score_prompt, score_self], -1)
    maxima = jnp.max(scores, -1, keepdims=True)
    exponent = jnp.exp(scores - maxima)
    weights = exponent / jnp.sum(exponent, -1, keepdims=True)
    weights_low = weights.astype(jnp.bfloat16)
    attended = product("rgip,pd->rigd", weights_low[..., :prompt_rows], value_prompt)
    attended = attended + product("rgij,rjd->rigd", weights_low[..., prompt_rows:], value_self)
    attended_low = (attended * row_mask[:, :, None, None]).astype(jnp.bfloat16)
    row_dot = jnp.sum(grad_head.astype(jnp.float32) * attended_low.astype(jnp.float32), -1)
    grad_weights = jnp.concatenate(
        [
            product("rigd,pd->rgip", grad_head, value_prompt),
            product("rigd,rjd->rgij", grad_head, value_self),
        ],
        -1,
    )
    score_grad = (weights * (grad_weights - jnp.transpose(row_dot, (0, 2, 1))[..., None])).astype(
        jnp.bfloat16
    )
    grad_prompt = score_grad[..., :prompt_rows]
    grad_self = score_grad[..., prompt_rows:]
    query_grad = (
        (
            product("rgip,pd->rigd", grad_prompt, key_prompt)
            + product("rgij,rjd->rigd", grad_self, key_self)
        )
        * scaling
    ).astype(jnp.bfloat16)
    selfkey_grad = (product("rgij,rigd->rjd", grad_self, query_head) * scaling).astype(jnp.bfloat16)
    selfval_grad = product("rgij,rigd->rjd", weights_low[..., prompt_rows:], grad_head).astype(
        jnp.bfloat16
    )
    promptk_grad = product("rgip,rigd->pd", grad_prompt, query_head) * scaling
    promptv_grad = product("rgip,rigd->pd", weights_low[..., :prompt_rows], grad_head)
    return (attended_low, query_grad, selfkey_grad, selfval_grad, promptk_grad, promptv_grad)


def on_device(
    queries,
    resp_keys,
    resp_values,
    out_grad,
    resp_lengths,
    prompt_keys,
    prompt_values,
    prompt_length,
):
    resp_count = queries.shape[0]
    resp_len = queries.shape[1]
    group_size = HEADS // KV_HEADS
    shard_rows = prompt_keys.shape[0]
    prompt_total = shard_rows * lax.axis_size("resp")
    live_prompt = jnp.arange(prompt_total) < prompt_length[0]
    positions = jnp.arange(resp_len)
    causal = positions[None, :] <= positions[:, None]
    row_mask = positions[None, :] < resp_lengths[:, None]
    masked_grad = out_grad * row_mask[:, :, None].astype(out_grad.dtype)
    query_heads = queries.reshape(resp_count, resp_len, KV_HEADS, group_size, HEAD_DIM).transpose(
        2, 0, 1, 3, 4
    )
    grad_heads = masked_grad.reshape(
        resp_count, resp_len, KV_HEADS, group_size, HEAD_DIM
    ).transpose(2, 0, 1, 3, 4)
    key_heads = resp_keys.reshape(resp_count, resp_len, KV_HEADS, HEAD_DIM).transpose(2, 0, 1, 3)
    value_heads = resp_values.reshape(resp_count, resp_len, KV_HEADS, HEAD_DIM).transpose(
        2, 0, 1, 3
    )
    gathered_keys, gathered_values = (
        lax.all_gather(prompt_keys, "resp", axis=0, tiled=True),
        lax.all_gather(prompt_values, "resp", axis=0, tiled=True),
    )
    pkey_heads = gathered_keys.reshape(prompt_total, KV_HEADS, HEAD_DIM).transpose(1, 0, 2)
    pval_heads = gathered_values.reshape(prompt_total, KV_HEADS, HEAD_DIM).transpose(1, 0, 2)

    def per_head(inputs):
        query_head, key_self, value_self, grad_head, key_prompt, value_prompt = inputs
        results = head_core(
            query_head,
            key_self,
            value_self,
            grad_head,
            key_prompt,
            value_prompt,
            live_prompt,
            causal,
            row_mask,
        )
        return results

    mapped = lax.map(
        per_head, (query_heads, key_heads, value_heads, grad_heads, pkey_heads, pval_heads)
    )
    attended = mapped[0].transpose(1, 2, 0, 3, 4).reshape(resp_count, resp_len, HEADS * HEAD_DIM)
    query_grad = mapped[1].transpose(1, 2, 0, 3, 4).reshape(resp_count, resp_len, HEADS * HEAD_DIM)
    selfkey_grad = (
        mapped[2].transpose(1, 2, 0, 3).reshape(resp_count, resp_len, KV_HEADS * HEAD_DIM)
    )
    selfval_grad = (
        mapped[3].transpose(1, 2, 0, 3).reshape(resp_count, resp_len, KV_HEADS * HEAD_DIM)
    )
    promptk_grad = mapped[4].transpose(1, 0, 2)
    promptv_grad = mapped[5].transpose(1, 0, 2)
    promptk_grad = promptk_grad.reshape(promptk_grad.shape[0], KV_HEADS * HEAD_DIM)
    promptv_grad = promptv_grad.reshape(promptv_grad.shape[0], KV_HEADS * HEAD_DIM)
    promptk_grad, promptv_grad = (
        lax.psum_scatter(promptk_grad, "resp", scatter_dimension=0, tiled=True),
        lax.psum_scatter(promptv_grad, "resp", scatter_dimension=0, tiled=True),
    )
    return (attended, query_grad, selfkey_grad, selfval_grad, promptk_grad, promptv_grad)


def solution(mesh):
    placed = (
        P(("groups", "resp"), None, None),
        P(("groups", "resp"), None, None),
        P(("groups", "resp"), None, None),
        P(("groups", "resp"), None, None),
        P(("groups", "resp")),
        P(("groups", "resp"), None),
        P(("groups", "resp"), None),
        P("groups"),
    )
    return jax.shard_map(
        on_device,
        mesh=mesh,
        in_specs=placed,
        out_specs=(
            P(("groups", "resp"), None, None),
            P(("groups", "resp"), None, None),
            P(("groups", "resp"), None, None),
            P(("groups", "resp"), None, None),
            P(("groups", "resp"), None),
            P(("groups", "resp"), None),
        ),
        check_vma=False,
    )
```

profile of v0, /device:TPU:0, one launch (start us, length us, event | category | flops | bytes accessed | tf_op | source)
XLA Modules:
  0.0 213.3 jit_solution(2638327750993567545)
XLA Ops:
  7.9 1.1 broadcast_multiply_fusion
  9.4 24.6 %all_gather.6 = bf16[512,512]{1,0:T(8,128)(2,1)S(1)} all-gather(bf16[32,512]{1,0:T(8,128)(2,1)S(1)} %copy-done.6), channel_id=1, replica_groups=mesh['groups'=2,'resp'=16] {'resp'}, dimensions={0}, use_global_device_ids=true | all-gather | bytes 557056 | tf_op jit(solution)/shard_map/all_gather | solution.py:101
  34.2 18.9 %all_gather.7 = bf16[512,512]{1,0:T(8,128)(2,1)S(1)} all-gather(bf16[32,512]{1,0:T(8,128)(2,1)S(1)} %copy-done.7), channel_id=1, replica_groups=mesh['groups'=2,'resp'=16] {'resp'}, dimensions={0}, use_global_device_ids=true | all-gather | bytes 557056 | tf_op jit(solution)/shard_map/all_gather | solution.py:100
  53.3 1.3 copy.66
  54.9 33.3 %while.21 = (s32[]{:T(128)}, bf16[4,1,128,4,128]{2,4,3,1,0:T(8,128)(2,1)}, bf16[4,1,128,4,128]{2,4,3,1,0:T(8,128)(2,1)}, bf16[4,1,128,128]{3,2,1,0:T(8,128)(2,1)...) while((s32[]{:T(128)}, ...), condition=%wide.region_5.6_spmd.clone, body=%wide.region_0.5_spmd.clone.sunk | while | flops 509672704 | bytes 15866025 | solution.py:121
  57.5 0.8 bitcast_dynamic-update-slice_fusion.2
  59.8 0.8 fusion.129
  61.4 1.0 fusion.133
  65.8 0.8 bitcast_dynamic-update-slice_fusion.2
  68.1 0.8 fusion.129
  69.8 1.0 fusion.133
  74.2 0.8 bitcast_dynamic-update-slice_fusion.2
  76.4 0.8 fusion.129
  78.1 1.0 fusion.133
  82.5 0.8 bitcast_dynamic-update-slice_fusion.2
  84.8 0.8 fusion.129
  86.4 1.0 fusion.133
  88.2 1.2 copy_bitcast_fusion.1
  89.5 2.4 %copy_bitcast_fusion = f32[512,512]{1,0:T(8,128)} fusion(f32[4,512,128]{2,1,0:T(8,128)} %get-tuple-element.98), kind=kLoop, calls=%fused_computation.102 | loop fusion | bytes 2097152 | tf_op jit(solution)/shard_map/reshape | solution.py:135
  91.8 1.0 copy-done
  92.9 1.0 copy.87
  93.9 1.0 copy.88
  95.6 49.8 %reduce-scatter.3.cloned.1.call-done = f32[32,512]{1,0:T(8,128)} async-done(((f32[512,512]{1,0:T(8,128)}), f32[32,512]{1,0:T(8,128)}) %reduce-scatter.3.cloned.1.call-update) | async-done | bytes 65552 | tf_op jit(solution)/shard_map/reduce_scatter | solution.py:137
  145.4 61.0 %reduce-scatter.5.cloned.1.call-done = f32[32,512]{1,0:T(8,128)} async-done(((f32[512,512]{1,0:T(8,128)}), f32[32,512]{1,0:T(8,128)}) %reduce-scatter.5.cloned.1.call-update) | async-done | bytes 65552 | tf_op jit(solution)/shard_map/reduce_scatter | solution.py:138
  (100 shorter events, 24.2 us)
Async XLA Ops:
  7.2 138.2 %reduce-scatter.3.cloned.1.call-start = ((), (), s32[]{:S(2)}) async-start(), calls=%async_computation.2 | async-start | bytes 1114112 | tf_op jit(solution)/shard_map/reduce_scatter | solution.py:137
  7.9 1.4 copy-start.6
  9.4 24.8 %copy-start.7 = (bf16[32,512]{1,0:T(8,128)(2,1)S(1)}, bf16[32,512]{1,0:T(8,128)(2,1)}, u32[]{:S(2)}) copy-start(bf16[32,512]{1,0:T(8,128)(2,1)} %param.15) | copy-start | bytes 98308
  53.1 1.5 copy-start.2
  53.1 1.7 copy-start.3
  89.4 117.0 %reduce-scatter.5.cloned.1.call-start = ((), (), s32[]{:S(2)}) async-start(), calls=%async_computation.3 | async-start | bytes 1114112 | tf_op jit(solution)/shard_map/reduce_scatter | solution.py:138
  91.8 1.0 copy-start
  91.8 2.1 copy-start.1
  92.9 2.0 copy-start.4
  92.9 2.0 copy-start.5
Sparse Core Ops, SparseCore 0:
  89.5 55.8 reduce-scatter.2
  150.0 56.3 reduce-scatter.4
where the time goes:
time: 214 us; the launch traced here: 213 us
  waiting for transfers between devices  111 us (52%)
  blocking collectives  43.5 us (20%)
  matrix products  24.6 us (11%)
  between operations  14.8 us (7%)
  other arithmetic  9.57 us (4%)
  local copies, waits for them, and re-layouts  9.55 us (4%)
    reduce_scatter x1, waiting for transfers between devices, on_device(): lax.psum_scatter(promptv_grad, 'resp', scatter_dimension=0, tiled=True)  61 us
    reduce_scatter x1, waiting for transfers between devices, on_device(): lax.psum_scatter(promptk_grad, 'resp', scatter_dimension=0, tiled=True)  49.8 us
    dot_general x48, matrix products, product(): return jnp.einsum(form, left, right, preferred_element_type=jnp.float32)  24.6 us
    all_gather x1, blocking collectives, on_device(): lax.all_gather(prompt_values, 'resp', axis=0, tiled=True)  24.6 us
    all_gather x1, blocking collectives, on_device(): lax.all_gather(prompt_keys, 'resp', axis=0, tiled=True)  18.9 us
  transfers between devices with their start and end apart: 2, of which 2 were waited for; matrix products, arithmetic and copies ran while one was open for 2% of the time, Pallas kernels for 0%

commit v1 on v0

v1 whole, which is shorter than its diff:
```python
import functools
import math

import jax
import jax.numpy as jnp
from jax import lax
from jax.experimental import pallas as pl
from jax.experimental.pallas import tpu as pltpu
from jax.sharding import PartitionSpec as P

HEADS = 16
KV_HEADS = 4
HEAD_DIM = 128
GROUP = HEADS // KV_HEADS
CORES = 2
PAIRS = 2
F32 = jnp.float32
BF16 = jnp.bfloat16


def nt(left, right):
    return lax.dot_general(left, right, (((1,), (1,)), ((), ())), preferred_element_type=F32)


def tn(left, right):
    return lax.dot_general(left, right, (((0,), (0,)), ((), ())), preferred_element_type=F32)


def nn(left, right):
    return lax.dot_general(left, right, (((1,), (0,)), ((), ())), preferred_element_type=F32)


def kernel(
    far,
    q_hbm, rk_ref, rv_ref, og_hbm, len_ref, pk_ref, pv_ref, plen_ref,
    o_hbm, dq_hbm, dk_ref, dv_ref, dpk_ref, dpv_ref,
    q, og, ob, dqb, held, part, from_core, core_sum, from_pair, pair_sum, from_far, bias,
    load_sem, store_sem,
    s1, r1, s2, r2, s3, r3, sa, ra, sb, rb, sc, rc,
):
    me = lax.axis_index("resp")
    c = lax.rem(me, CORES)
    y = lax.rem(lax.div(me, CORES), PAIRS)
    z = lax.div(me, CORES * PAIRS)
    rows = pk_ref.shape[0]
    prompt = rows * far * PAIRS * CORES
    length = q_hbm.shape[1]
    wide = GROUP * length
    scaling = HEAD_DIM ** -0.5

    def device(zz, yy, cc):
        return {"resp": (zz * PAIRS + yy) * CORES + cc}

    def remote(src, dst, send, recv, target):
        return pltpu.make_async_remote_copy(
            src_ref=src, dst_ref=dst, send_sem=send, recv_sem=recv,
            device_id=target, device_id_type=pl.DeviceIdType.MESH,
        )

    def ahead(d):
        return lax.rem(z + d, far)

    def behind(d):
        return lax.rem(z + (far - d), far)

    pair_dev = device(z, 1 - y, c)
    core_dev = device(z, y, 1 - c)

    q_load = pltpu.make_async_copy(q_hbm.at[0], q, load_sem.at[0])
    og_load = pltpu.make_async_copy(og_hbm.at[0], og, load_sem.at[1])
    q_load.start()
    og_load.start()

    barrier = pltpu.get_barrier_semaphore()
    for d in range(1, far):
        pl.semaphore_signal(barrier, inc=1, device_id=device(ahead(d), y, c),
                            device_id_type=pl.DeviceIdType.MESH)
    pl.semaphore_signal(barrier, inc=1, device_id=pair_dev, device_id_type=pl.DeviceIdType.MESH)
    pl.semaphore_signal(barrier, inc=1, device_id=core_dev, device_id_type=pl.DeviceIdType.MESH)

    for h in range(KV_HEADS):
        lanes = slice(h * HEAD_DIM, (h + 1) * HEAD_DIM)
        held[h, c, y, z, :, :HEAD_DIM] = pk_ref[:, lanes]
        held[h, c, y, z, :, HEAD_DIM:] = pv_ref[:, lanes]

    pl.semaphore_wait(barrier, far + 1)

    def gather_far(h, d, slot):
        return remote(held.at[h, c, y, slot], held.at[h, c, y, slot],
                      s1.at[h, d - 1], r1.at[h, d - 1], device(ahead(d), y, c))

    def gather_pair(h, yy):
        return remote(held.at[h, c, yy], held.at[h, c, yy], s2.at[h], r2.at[h], pair_dev)

    def gather_core(h, cc):
        return remote(held.at[h, cc], held.at[h, cc], s3.at[h], r3.at[h], core_dev)

    def pass_pair(h):
        for d in range(1, far):
            gather_far(h, d, behind(d)).wait_recv()
        gather_pair(h, y).start()

    def pass_core(h):
        gather_pair(h, 1 - y).wait_recv()
        gather_core(h, c).start()

    def reduce_core(h):
        return remote(part.at[h, 1 - c], from_core.at[h], sa.at[h], ra.at[h], core_dev)

    def reduce_pair(h):
        return remote(core_sum.at[h, 1 - y], from_pair.at[h], sb.at[h], rb.at[h], pair_dev)

    def reduce_far(h, d):
        return remote(pair_sum.at[h, ahead(d)], from_far.at[h, d - 1],
                      sc.at[h, d - 1], rc.at[h, d - 1], device(ahead(d), y, c))

    def add_core(h):
        reduce_core(h).wait_recv()
        core_sum[h] = (part[h, c].astype(F32) + from_core[h].astype(F32)).astype(BF16)
        reduce_pair(h).start()

    def add_pair(h):
        reduce_pair(h).wait_recv()
        pair_sum[h] = (core_sum[h, y].astype(F32) + from_pair[h].astype(F32)).astype(BF16)
        for d in range(1, far):
            reduce_far(h, d).start()

    def add_far(h):
        total = pair_sum[h, z].astype(F32)
        for d in range(1, far):
            reduce_far(h, d).wait_recv()
            total = total + from_far[h, d - 1].astype(F32)
        lanes = slice(h * HEAD_DIM, (h + 1) * HEAD_DIM)
        dpk_ref[:, lanes] = total[:, :HEAD_DIM] * scaling
        dpv_ref[:, lanes] = total[:, HEAD_DIM:]

    for h in range(KV_HEADS):
        for d in range(1, far):
            gather_far(h, d, z).start()

    index = lax.broadcasted_iota(jnp.int32, (prompt, length), 0)
    block = lax.div(index, rows)
    owner = (
        lax.rem(block, far) * (PAIRS * CORES)
        + lax.rem(lax.div(block, far), PAIRS) * CORES
        + lax.div(block, far * PAIRS)
    )
    position = owner * rows + lax.rem(index, rows)
    bias[...] = jnp.where(position < plen_ref[0], 0.0, -jnp.inf)
    below = lax.broadcasted_iota(jnp.int32, (length, length), 0)
    after = lax.broadcasted_iota(jnp.int32, (length, length), 1)
    causal = jnp.where(below <= after, 0.0, -jnp.inf)
    live = below < len_ref[0]

    def out_store(h):
        lanes = pl.ds(h * GROUP * HEAD_DIM, GROUP * HEAD_DIM)
        return pltpu.make_async_copy(ob.at[:, lanes], o_hbm.at[0, :, lanes], store_sem.at[0, h])

    def dq_store(h):
        lanes = pl.ds(h * GROUP * HEAD_DIM, GROUP * HEAD_DIM)
        return pltpu.make_async_copy(dqb.at[:, lanes], dq_hbm.at[0, :, lanes], store_sem.at[1, h])

    def head_lanes(h, i):
        return slice((h * GROUP + i) * HEAD_DIM, (h * GROUP + i + 1) * HEAD_DIM)

    def compute(h):
        lanes = slice(h * HEAD_DIM, (h + 1) * HEAD_DIM)
        key_self, value_self = rk_ref[0, :, lanes], rv_ref[0, :, lanes]
        query = jnp.concatenate([q[:, head_lanes(h, i)] for i in range(GROUP)], 0)
        grad = jnp.concatenate(
            [jnp.where(live, og[:, head_lanes(h, i)], jnp.zeros((), BF16)) for i in range(GROUP)], 0
        )
        both = held[h].reshape(prompt, 2 * HEAD_DIM)
        key, value = both[:, :HEAD_DIM], both[:, HEAD_DIM:]
        masks = jnp.concatenate([bias[...]] * GROUP, 1)
        causals = jnp.concatenate([causal] * GROUP, 1)
        score_p = nt(key, query) + masks
        score_s = nt(key_self, query) + causals
        top = jnp.maximum(
            jnp.max(score_p, 0, keepdims=True), jnp.max(score_s, 0, keepdims=True)
        )
        factor = scaling * math.log2(math.e)
        exp_p = jnp.exp2((score_p - top) * factor)
        exp_s = jnp.exp2((score_s - top) * factor)
        inverse = 1.0 / (jnp.sum(exp_p, 0, keepdims=True) + jnp.sum(exp_s, 0, keepdims=True))
        weight_p, weight_s = exp_p * inverse, exp_s * inverse
        low_p, low_s = weight_p.astype(BF16), weight_s.astype(BF16)
        part_v = nn(low_p, grad)
        gw_p, gw_s = nt(value, grad), nt(value_self, grad)
        dot = jnp.sum(weight_p * gw_p, 0, keepdims=True) + jnp.sum(weight_s * gw_s, 0, keepdims=True)
        sg_p = (weight_p * (gw_p - dot)).astype(BF16)
        sg_s = (weight_s * (gw_s - dot)).astype(BF16)
        part_k = nn(sg_p, query)
        shape = (CORES, PAIRS, far, rows, HEAD_DIM)
        part[h, :, :, :, :, :HEAD_DIM] = part_k.astype(BF16).reshape(shape)
        part[h, :, :, :, :, HEAD_DIM:] = part_v.astype(BF16).reshape(shape)
        reduce_core(h).start()
        out_t = tn(value, low_p) + tn(value_self, low_s)
        dq_t = (tn(key, sg_p) + tn(key_self, sg_s)) * scaling
        for i in range(GROUP):
            cut = slice(i * length, (i + 1) * length)
            ob[:, head_lanes(h, i)] = jnp.where(live, out_t[:, cut].T, 0.0).astype(BF16)
            dqb[:, head_lanes(h, i)] = dq_t[:, cut].T.astype(BF16)
        out_store(h).start()
        dq_store(h).start()
        dk_ref[0, :, lanes] = (nn(sg_s, query) * scaling).astype(BF16)
        dv_ref[0, :, lanes] = nn(low_s, grad).astype(BF16)

    last = KV_HEADS - 1
    pass_pair(0)
    pass_pair(1)
    pass_core(0)
    pass_pair(2)
    pass_core(1)
    pass_pair(3)
    q_load.wait()
    og_load.wait()
    for h in range(KV_HEADS):
        if h == 1:
            pass_core(2)
            pass_core(3)
        gather_core(h, 1 - c).wait_recv()
        compute(h)
        if h >= 1:
            add_core(h - 1)
        if h >= 2:
            add_pair(h - 2)
    add_core(last)
    add_pair(last - 1)
    for h in range(last):
        add_far(h)
    add_pair(last)
    for h in range(KV_HEADS):
        out_store(h).wait()
        dq_store(h).wait()
        for d in range(1, far):
            gather_far(h, d, z).wait_send()
        gather_pair(h, y).wait_send()
        gather_core(h, c).wait_send()
        reduce_core(h).wait_send()
        reduce_pair(h).wait_send()
    add_far(last)
    for h in range(KV_HEADS):
        for d in range(1, far):
            reduce_far(h, d).wait_send()


def on_device(far, queries, resp_keys, resp_values, out_grad, resp_lengths, prompt_keys, prompt_values, prompt_length):
    length, width = queries.shape[1:]
    rows, kv_width = prompt_keys.shape
    prompt = rows * far * PAIRS * CORES
    any_spec = pl.BlockSpec(memory_space=pl.ANY)
    vmem = pl.BlockSpec(memory_space=pltpu.VMEM)
    smem = pl.BlockSpec(memory_space=pltpu.SMEM)
    both = 2 * HEAD_DIM
    dma = pltpu.SemaphoreType.DMA
    return pl.pallas_call(
        functools.partial(kernel, far),
        out_shape=(
            jax.ShapeDtypeStruct(queries.shape, BF16),
            jax.ShapeDtypeStruct(queries.shape, BF16),
            jax.ShapeDtypeStruct(resp_keys.shape, BF16),
            jax.ShapeDtypeStruct(resp_keys.shape, BF16),
            jax.ShapeDtypeStruct(prompt_keys.shape, F32),
            jax.ShapeDtypeStruct(prompt_keys.shape, F32),
        ),
        in_specs=[any_spec, vmem, vmem, any_spec, smem, vmem, vmem, smem],
        out_specs=(any_spec, any_spec, vmem, vmem, vmem, vmem),
        scratch_shapes=[
            pltpu.VMEM((length, width), BF16),
            pltpu.VMEM((length, width), BF16),
            pltpu.VMEM((length, width), BF16),
            pltpu.VMEM((length, width), BF16),
            pltpu.VMEM((KV_HEADS, CORES, PAIRS, far, rows, both), BF16),
            pltpu.VMEM((KV_HEADS, CORES, PAIRS, far, rows, both), BF16),
            pltpu.VMEM((KV_HEADS, PAIRS, far, rows, both), BF16),
            pltpu.VMEM((KV_HEADS, PAIRS, far, rows, both), BF16),
            pltpu.VMEM((KV_HEADS, far, rows, both), BF16),
            pltpu.VMEM((KV_HEADS, far, rows, both), BF16),
            pltpu.VMEM((KV_HEADS, far - 1, rows, both), BF16),
            pltpu.VMEM((prompt, length), F32),
            dma((2,)),
            dma((2, KV_HEADS)),
            dma((KV_HEADS, far - 1)), dma((KV_HEADS, far - 1)),
            dma((KV_HEADS,)), dma((KV_HEADS,)),
            dma((KV_HEADS,)), dma((KV_HEADS,)),
            dma((KV_HEADS,)), dma((KV_HEADS,)),
            dma((KV_HEADS,)), dma((KV_HEADS,)),
            dma((KV_HEADS, far - 1)), dma((KV_HEADS, far - 1)),
        ],
        compiler_params=pltpu.CompilerParams(
            collective_id=0, has_side_effects=True, vmem_limit_bytes=60 * 1024 * 1024
        ),
    )(queries, resp_keys, resp_values, out_grad, resp_lengths, prompt_keys, prompt_values, prompt_length)


def solution(mesh):
    far = mesh.shape["resp"] // (CORES * PAIRS)
    shard = P(("groups", "resp"), None, None)
    flat = P(("groups", "resp"), None)
    return jax.shard_map(
        functools.partial(on_device, far),
        mesh=mesh,
        in_specs=(shard, shard, shard, shard, P(("groups", "resp")), flat, flat, P("groups")),
        out_specs=(shard, shard, shard, shard, flat, flat),
        check_vma=False,
    )
```

time: 214 us -> 46.4 us (0.22)
  waiting for transfers between devices: 111 us -> 0 us
  blocking collectives: 43.5 us -> 0 us
  Pallas kernels: 0 us -> 37.9 us
  matrix products: 24.6 us -> 0 us
  between operations: 14.8 us -> 1.95 us
  other arithmetic: 9.57 us -> 0 us
  local copies, waits for them, and re-layouts: 9.55 us -> 6.27 us
    reduce_scatter x2 -> x0, waiting for transfers between devices: 111 us -> none  [the longest x1 61 us: on_device(): lax.psum_scatter(promptv_grad, 'resp', scatter_dimension=0, tiled=True)]
    all_gather x2 -> x0, blocking collectives: 43.5 us -> none  [the longest x1 24.6 us: on_device(): lax.all_gather(prompt_values, 'resp', axis=0, tiled=True)]
    pallas_call x0 -> x1, Pallas kernels: none -> 37.9 us  [on_device(): pl.pallas_call(functools.partial(kernel, far), out_shape=(jax.ShapeDtypeS...]
    dot_general x48 -> x0, matrix products: 24.6 us -> none  [product(): return jnp.einsum(form, left, right, preferred_element_type=jnp.float32)]
    reshape x5 -> x0, local copies, waits for them, and re-layouts: 6.26 us -> none  [the longest x1 2.35 us: on_device(): promptv_grad.reshape(promptv_grad.shape[0], KV_HEADS * HEAD_DIM)]
    convert_element_type x13 -> x0, other arithmetic: 4.75 us -> none  [the longest x4 2.6 us: head_core(): attended_low = (attended * row_mask[:, :, None, None]).astype(jnp.bfloat16)]
    unnamed x19 -> x16, local copies, waits for them, and re-layouts: 2.59 us -> 6.27 us
    lt x4 -> x0, other arithmetic: 2.6 us -> none  [on_device(): live_prompt = jnp.arange(prompt_total) < prompt_length[0]]
  transfers between devices with their start and end apart: 2 -> 0, of which waited for: 2 -> 0; matrix products, arithmetic and copies ran while one was open for 2% -> 0% of each run, Pallas kernels for 0% -> 0%
where the time goes in v1:
time: 46.4 us; the launch traced here: 46.1 us
  Pallas kernels  37.9 us (82%)
  local copies, waits for them, and re-layouts  6.27 us (14%)
  between operations  1.95 us (4%)
    pallas_call x1, Pallas kernels, on_device(): pl.pallas_call(functools.partial(kernel, far), out_shape=(jax.ShapeDtypeS...  37.9 us
    unnamed x16, local copies, waits for them, and re-layouts  6.27 us

profile of v1, /device:TPU:0, one launch (start us, length us, event | category | flops | bytes accessed | tf_op | source)
XLA Modules:
  0.0 46.1 jit_solution(15520012604722189340)
XLA Ops:
  1.9 37.9 %shard_map.127 = (bf16[1,128,2048]{2,1,0:T(8,128)(2,1)}, bf16[1,128,2048]{2,1,0:T(8,128)(2,1)}, bf16[1,128,512]{2,1,0:T(8,128)(2,1)}, bf16[1,128,512]{2,1,0:T(8,...) custom-call(bf16[1,128,2048]{2,1,0:T(8,128)(2,1)} %q_hbm.1, bf16[1,128,512]{2,1,0:T(8,128)(2,1)} %rk_ref.1, ...), custom_call_target="tpu_custom_call" | custom-call | tf_op jit(solution)/shard_map/pallas_call | solution.py:257
  39.8 0.0 copy-start
  39.8 1.9 %copy.22 = bf16[1,128,2048]{2,1,0:T(8,128)(2,1)} copy(bf16[1,128,2048]{2,1,0:T(8,128)(2,1)} %get-tuple-element.12) | data formatting | bytes 1048576
  41.7 0.0 copy-done
  41.7 0.0 copy-start.2
  41.7 0.8 %copy.23 = bf16[1,128,2048]{2,1,0:T(8,128)(2,1)} copy(bf16[1,128,2048]{2,1,0:T(8,128)(2,1)S(1)} %copy-done) | data formatting | bytes 1048576
  42.5 0.2 copy-done.2
  42.8 0.0 copy-start.1
  42.8 0.7 %copy.24 = bf16[1,128,512]{2,1,0:T(8,128)(2,1)} copy(bf16[1,128,512]{2,1,0:T(8,128)(2,1)S(1)} %copy-done.2) | data formatting | bytes 262144
  43.4 0.3 copy-done.1
  43.7 0.0 copy-start.4
  43.7 0.7 %copy.25 = bf16[1,128,512]{2,1,0:T(8,128)(2,1)} copy(bf16[1,128,512]{2,1,0:T(8,128)(2,1)S(1)} %copy-done.1) | data formatting | bytes 262144
  44.4 0.2 copy-done.4
  44.6 0.0 copy-start.3
  44.6 0.6 %copy.26 = f32[32,512]{1,0:T(8,128)} copy(f32[32,512]{1,0:T(8,128)S(1)} %copy-done.4) | data formatting | bytes 131072
  45.2 0.2 copy-done.3
  45.4 0.6 %copy.27 = f32[32,512]{1,0:T(8,128)} copy(f32[32,512]{1,0:T(8,128)S(1)} %copy-done.3) | data formatting | bytes 131072
Async XLA Ops:
  39.8 2.0 %copy-start = (bf16[1,128,2048]{2,1,0:T(8,128)(2,1)S(1)}, bf16[1,128,2048]{2,1,0:T(8,128)(2,1)}, u32[]{:S(2)}) copy-start(bf16[1,128,2048]{2,1,0:T(8,128)(2,1)} %get-tuple-element.13) | copy-start | bytes 1572868
  41.7 1.0 %copy-start.2 = (bf16[1,128,512]{2,1,0:T(8,128)(2,1)S(1)}, bf16[1,128,512]{2,1,0:T(8,128)(2,1)}, u32[]{:S(2)}) copy-start(bf16[1,128,512]{2,1,0:T(8,128)(2,1)} %get-tuple-element.14) | copy-start | bytes 393220
  42.8 1.0 %copy-start.1 = (bf16[1,128,512]{2,1,0:T(8,128)(2,1)S(1)}, bf16[1,128,512]{2,1,0:T(8,128)(2,1)}, u32[]{:S(2)}) copy-start(bf16[1,128,512]{2,1,0:T(8,128)(2,1)} %get-tuple-element.15) | copy-start | bytes 393220
  43.7 0.9 %copy-start.4 = (f32[32,512]{1,0:T(8,128)S(1)}, f32[32,512]{1,0:T(8,128)}, u32[]{:S(2)}) copy-start(f32[32,512]{1,0:T(8,128)} %get-tuple-element.16) | copy-start | bytes 196612
  44.6 0.9 %copy-start.3 = (f32[32,512]{1,0:T(8,128)S(1)}, f32[32,512]{1,0:T(8,128)}, u32[]{:S(2)}) copy-start(f32[32,512]{1,0:T(8,128)} %get-tuple-element.17) | copy-start | bytes 196612

commit v2 on v1

v2 whole, which is shorter than its diff:
```python
import functools
import math

import jax
import jax.numpy as jnp
from jax import lax
from jax.experimental import pallas as pl
from jax.experimental.pallas import tpu as pltpu
from jax.sharding import PartitionSpec as P

HEADS = 16
KV_HEADS = 4
HEAD_DIM = 128
GROUP = HEADS // KV_HEADS
CORES = 2
PAIRS = 2
F32 = jnp.float32
BF16 = jnp.bfloat16


def nt(left, right):
    return lax.dot_general(left, right, (((1,), (1,)), ((), ())), preferred_element_type=F32)


def tn(left, right):
    return lax.dot_general(left, right, (((0,), (0,)), ((), ())), preferred_element_type=F32)


def nn(left, right):
    return lax.dot_general(left, right, (((1,), (0,)), ((), ())), preferred_element_type=F32)


def kernel(
    far,
    q_hbm, rk_hbm, rv_hbm, og_hbm, len_ref, pk_hbm, pv_hbm, plen_ref,
    o_ref, dq_ref, dk_ref, dv_ref, dpk_ref, dpv_ref,
    q, og, rk, rv, pk, pv, held, part, from_core, core_sum, from_pair, pair_sum, from_far, bias,
    load_sem,
    s1, r1, s2, r2, s3, r3, sa, ra, sb, rb, sc, rc,
):
    me = lax.axis_index("resp")
    c = lax.rem(me, CORES)
    y = lax.rem(lax.div(me, CORES), PAIRS)
    z = lax.div(me, CORES * PAIRS)
    rows = pk_hbm.shape[0]
    prompt = rows * far * PAIRS * CORES
    length = q_hbm.shape[1]
    wide = GROUP * length
    scaling = HEAD_DIM ** -0.5

    def device(zz, yy, cc):
        return {"resp": (zz * PAIRS + yy) * CORES + cc}

    def remote(src, dst, send, recv, target):
        return pltpu.make_async_remote_copy(
            src_ref=src, dst_ref=dst, send_sem=send, recv_sem=recv,
            device_id=target, device_id_type=pl.DeviceIdType.MESH,
        )

    def ahead(d):
        return lax.rem(z + d, far)

    def behind(d):
        return lax.rem(z + (far - d), far)

    pair_dev = device(z, 1 - y, c)
    core_dev = device(z, y, 1 - c)

    loads = [
        pltpu.make_async_copy(src, dst, load_sem.at[i])
        for i, (src, dst) in enumerate((
            (pk_hbm, pk), (pv_hbm, pv), (rk_hbm.at[0], rk), (rv_hbm.at[0], rv),
            (q_hbm.at[0], q), (og_hbm.at[0], og),
        ))
    ]
    for load in loads:
        load.start()

    barrier = pltpu.get_barrier_semaphore()
    for d in range(1, far):
        pl.semaphore_signal(barrier, inc=1, device_id=device(ahead(d), y, c),
                            device_id_type=pl.DeviceIdType.MESH)
    pl.semaphore_signal(barrier, inc=1, device_id=pair_dev, device_id_type=pl.DeviceIdType.MESH)
    pl.semaphore_signal(barrier, inc=1, device_id=core_dev, device_id_type=pl.DeviceIdType.MESH)

    loads[0].wait()
    loads[1].wait()
    for h in range(KV_HEADS):
        lanes = slice(h * HEAD_DIM, (h + 1) * HEAD_DIM)
        held[h, c, y, z, :, :HEAD_DIM] = pk[:, lanes]
        held[h, c, y, z, :, HEAD_DIM:] = pv[:, lanes]

    pl.semaphore_wait(barrier, far + 1)

    def gather_far(h, d, slot):
        return remote(held.at[h, c, y, slot], held.at[h, c, y, slot],
                      s1.at[h, d - 1], r1.at[h, d - 1], device(ahead(d), y, c))

    def gather_pair(h, d, yy):
        slot = behind(d)
        return remote(held.at[h, c, yy, slot], held.at[h, c, yy, slot],
                      s2.at[h, d], r2.at[h, d], pair_dev)

    def gather_core(h, cc):
        return remote(held.at[h, cc], held.at[h, cc], s3.at[h], r3.at[h], core_dev)

    def start_far(h):
        for d in range(1, far):
            gather_far(h, d, z).start()
        gather_pair(h, 0, y).start()

    def pass_pair(h):
        for d in range(1, far):
            gather_far(h, d, behind(d)).wait_recv()
            gather_pair(h, d, y).start()

    def pass_core(h):
        for d in range(far):
            gather_pair(h, d, 1 - y).wait_recv()
        gather_core(h, c).start()

    steps = [*range(1, far), 0]

    def reduce_core(h):
        return remote(part.at[h, 1 - c], from_core.at[h], sa.at[h], ra.at[h], core_dev)

    def reduce_pair(h, d):
        slot = ahead(d)
        return remote(core_sum.at[h, slot], from_pair.at[h, slot], sb.at[h, d], rb.at[h, d], pair_dev)

    def reduce_far(h, d):
        return remote(pair_sum.at[h, d - 1], from_far.at[h, d - 1],
                      sc.at[h, d - 1], rc.at[h, d - 1], device(ahead(d), y, c))

    def add_core(h):
        reduce_core(h).wait_recv()
        for d in steps:
            slot = ahead(d)
            core_sum[h, slot] = (
                part[h, c, 1 - y, slot].astype(F32) + from_core[h, 1 - y, slot].astype(F32)
            ).astype(BF16)
            reduce_pair(h, d).start()

    def own_sum(h, d):
        slot = ahead(d)
        reduce_pair(h, d).wait_recv()
        return (
            part[h, c, y, slot].astype(F32)
            + from_core[h, y, slot].astype(F32)
            + from_pair[h, slot].astype(F32)
        )

    def add_pair(h):
        for d in range(1, far):
            pair_sum[h, d - 1] = own_sum(h, d).astype(BF16)
            reduce_far(h, d).start()

    def add_far(h):
        total = own_sum(h, 0)
        for d in range(1, far):
            reduce_far(h, d).wait_recv()
            total = total + from_far[h, d - 1].astype(F32)
        lanes = slice(h * HEAD_DIM, (h + 1) * HEAD_DIM)
        dpk_ref[:, lanes] = total[:, :HEAD_DIM] * scaling
        dpv_ref[:, lanes] = total[:, HEAD_DIM:]

    start_far(0)
    start_far(1)

    index = lax.broadcasted_iota(jnp.int32, (prompt, length), 0)
    block = lax.div(index, rows)
    owner = (
        lax.rem(block, far) * (PAIRS * CORES)
        + lax.rem(lax.div(block, far), PAIRS) * CORES
        + lax.div(block, far * PAIRS)
    )
    position = owner * rows + lax.rem(index, rows)
    bias[...] = jnp.where(position < plen_ref[0], 0.0, -jnp.inf)
    below = lax.broadcasted_iota(jnp.int32, (length, length), 0)
    after = lax.broadcasted_iota(jnp.int32, (length, length), 1)
    causal = jnp.where(below <= after, 0.0, -jnp.inf)
    live = below < len_ref[0]

    def head_lanes(h, i):
        return slice((h * GROUP + i) * HEAD_DIM, (h * GROUP + i + 1) * HEAD_DIM)

    def compute(h, between):
        lanes = slice(h * HEAD_DIM, (h + 1) * HEAD_DIM)
        key_self, value_self = rk[:, lanes], rv[:, lanes]
        query = jnp.concatenate([q[:, head_lanes(h, i)] for i in range(GROUP)], 0)
        grad = jnp.concatenate(
            [jnp.where(live, og[:, head_lanes(h, i)], jnp.zeros((), BF16)) for i in range(GROUP)], 0
        )
        both = held[h].reshape(prompt, 2 * HEAD_DIM)
        key, value = both[:, :HEAD_DIM], both[:, HEAD_DIM:]
        masks = jnp.concatenate([bias[...]] * GROUP, 1)
        causals = jnp.concatenate([causal] * GROUP, 1)
        score_p = nt(key, query) + masks
        score_s = nt(key_self, query) + causals
        top = jnp.maximum(
            jnp.max(score_p, 0, keepdims=True), jnp.max(score_s, 0, keepdims=True)
        )
        factor = scaling * math.log2(math.e)
        exp_p = jnp.exp2((score_p - top) * factor)
        exp_s = jnp.exp2((score_s - top) * factor)
        inverse = 1.0 / (jnp.sum(exp_p, 0, keepdims=True) + jnp.sum(exp_s, 0, keepdims=True))
        weight_p, weight_s = exp_p * inverse, exp_s * inverse
        low_p, low_s = weight_p.astype(BF16), weight_s.astype(BF16)
        part_v = nn(low_p, grad)
        gw_p, gw_s = nt(value, grad), nt(value_self, grad)
        dot = jnp.sum(weight_p * gw_p, 0, keepdims=True) + jnp.sum(weight_s * gw_s, 0, keepdims=True)
        sg_p = (weight_p * (gw_p - dot)).astype(BF16)
        sg_s = (weight_s * (gw_s - dot)).astype(BF16)
        part_k = nn(sg_p, query)
        shape = (CORES, PAIRS, far, rows, HEAD_DIM)
        part[h, :, :, :, :, :HEAD_DIM] = part_k.astype(BF16).reshape(shape)
        part[h, :, :, :, :, HEAD_DIM:] = part_v.astype(BF16).reshape(shape)
        reduce_core(h).start()
        between()
        out_t = tn(value, low_p) + tn(value_self, low_s)
        dq_t = (tn(key, sg_p) + tn(key_self, sg_s)) * scaling
        for i in range(GROUP):
            cut = slice(i * length, (i + 1) * length)
            o_ref[0, :, head_lanes(h, i)] = jnp.where(live, out_t[:, cut].T, 0.0).astype(BF16)
            dq_ref[0, :, head_lanes(h, i)] = dq_t[:, cut].T.astype(BF16)
        dk_ref[0, :, lanes] = (nn(sg_s, query) * scaling).astype(BF16)
        dv_ref[0, :, lanes] = nn(low_s, grad).astype(BF16)

    last = KV_HEADS - 1
    pass_pair(0)
    start_far(2)
    pass_pair(1)
    start_far(3)
    pass_core(0)
    for load in loads[2:]:
        load.wait()

    def between(h):
        if h == 0:
            pass_pair(2)
            pass_core(1)
        if h == 1:
            pass_core(2)
        if h >= 1:
            add_pair(h - 1)

    for h in range(KV_HEADS):
        gather_core(h, 1 - c).wait_recv()
        compute(h, functools.partial(between, h))
        if h == 0:
            pass_pair(3)
        if h == 1:
            pass_core(3)
        add_core(h)
    add_far(0)
    add_pair(last)
    for h in range(1, last):
        add_far(h)
    for h in range(KV_HEADS):
        for d in range(1, far):
            gather_far(h, d, z).wait_send()
        for d in range(far):
            gather_pair(h, d, y).wait_send()
            reduce_pair(h, d).wait_send()
        gather_core(h, c).wait_send()
        reduce_core(h).wait_send()
    add_far(last)
    for h in range(KV_HEADS):
        for d in range(1, far):
            reduce_far(h, d).wait_send()


def store_kernel(*refs):
    count = len(refs) // 2
    sems = refs[-1]
    copies = [pltpu.make_async_copy(refs[i], refs[count + i], sems.at[i]) for i in range(count)]
    for copy in copies:
        copy.start()
    for copy in copies:
        copy.wait()


def on_device(far, queries, resp_keys, resp_values, out_grad, resp_lengths, prompt_keys, prompt_values, prompt_length):
    length, width = queries.shape[1:]
    rows, kv_width = prompt_keys.shape
    prompt = rows * far * PAIRS * CORES
    any_spec = pl.BlockSpec(memory_space=pltpu.HBM)
    vmem = pl.BlockSpec(memory_space=pltpu.VMEM)
    smem = pl.BlockSpec(memory_space=pltpu.SMEM)
    both = 2 * HEAD_DIM
    dma = pltpu.SemaphoreType.DMA
    results = pl.pallas_call(
        functools.partial(kernel, far),
        out_shape=(
            pltpu.VMEM(queries.shape, BF16),
            pltpu.VMEM(queries.shape, BF16),
            pltpu.VMEM(resp_keys.shape, BF16),
            pltpu.VMEM(resp_keys.shape, BF16),
            pltpu.VMEM(prompt_keys.shape, F32),
            pltpu.VMEM(prompt_keys.shape, F32),
        ),
        in_specs=[any_spec, any_spec, any_spec, any_spec, smem, any_spec, any_spec, smem],
        out_specs=(vmem,) * 6,
        scratch_shapes=[
            pltpu.VMEM((length, width), BF16),
            pltpu.VMEM((length, width), BF16),
            pltpu.VMEM((length, kv_width), BF16),
            pltpu.VMEM((length, kv_width), BF16),
            pltpu.VMEM((rows, kv_width), BF16),
            pltpu.VMEM((rows, kv_width), BF16),
            pltpu.VMEM((KV_HEADS, CORES, PAIRS, far, rows, both), BF16),
            pltpu.VMEM((KV_HEADS, CORES, PAIRS, far, rows, both), BF16),
            pltpu.VMEM((KV_HEADS, PAIRS, far, rows, both), BF16),
            pltpu.VMEM((KV_HEADS, far, rows, both), BF16),
            pltpu.VMEM((KV_HEADS, far, rows, both), BF16),
            pltpu.VMEM((KV_HEADS, far - 1, rows, both), BF16),
            pltpu.VMEM((KV_HEADS, far - 1, rows, both), BF16),
            pltpu.VMEM((prompt, length), F32),
            dma((6,)),
            dma((KV_HEADS, far - 1)), dma((KV_HEADS, far - 1)),
            dma((KV_HEADS, far)), dma((KV_HEADS, far)),
            dma((KV_HEADS,)), dma((KV_HEADS,)),
            dma((KV_HEADS,)), dma((KV_HEADS,)),
            dma((KV_HEADS, far)), dma((KV_HEADS, far)),
            dma((KV_HEADS, far - 1)), dma((KV_HEADS, far - 1)),
        ],
        compiler_params=pltpu.CompilerParams(
            collective_id=0, has_side_effects=True, vmem_limit_bytes=62 * 1024 * 1024
        ),
    )(queries, resp_keys, resp_values, out_grad, resp_lengths, prompt_keys, prompt_values, prompt_length)
    return pl.pallas_call(
        store_kernel,
        out_shape=tuple(jax.ShapeDtypeStruct(x.shape, x.dtype) for x in results),
        in_specs=[vmem] * 6,
        out_specs=(any_spec,) * 6,
        scratch_shapes=[dma((6,))],
        compiler_params=pltpu.CompilerParams(vmem_limit_bytes=2 * 1024 * 1024),
    )(*results)


def solution(mesh):
    far = mesh.shape["resp"] // (CORES * PAIRS)
    shard = P(("groups", "resp"), None, None)
    flat = P(("groups", "resp"), None)
    return jax.shard_map(
        functools.partial(on_device, far),
        mesh=mesh,
        in_specs=(shard, shard, shard, shard, P(("groups", "resp")), flat, flat, P("groups")),
        out_specs=(shard, shard, shard, shard, flat, flat),
        check_vma=False,
    )
```

time: 46.4 us -> 38.8 us (0.84)
  local copies, waits for them, and re-layouts: 6.27 us -> 0 us
  Pallas kernels: 37.9 us -> 36.7 us
    unnamed x16 -> x0, local copies, waits for them, and re-layouts: 6.27 us -> none
    pallas_call x1 -> x2, Pallas kernels: 37.9 us -> 36.7 us  [the longest x1 35.6 us: on_device(): pl.pallas_call(functools.partial(kernel, far), out_shape=(pltpu.VMEM(quer...]
where the time goes in v2:
time: 38.8 us; the launch traced here: 38.6 us
  Pallas kernels  36.7 us (95%)
  between operations  1.93 us (5%)
    pallas_call x1, Pallas kernels, on_device(): pl.pallas_call(functools.partial(kernel, far), out_shape=(pltpu.VMEM(quer...  35.6 us
    pallas_call x1, Pallas kernels, on_device(): pl.pallas_call(store_kernel, out_shape=tuple((jax.ShapeDtypeStruct(x.shap...  1.14 us

profile of v2, /device:TPU:0, one launch (start us, length us, event | category | flops | bytes accessed | tf_op | source)
XLA Modules:
  0.0 38.6 jit_solution(6678127401036953750)
XLA Ops:
  1.9 35.6 %shard_map.127 = (bf16[1,128,2048]{2,1,0:T(8,128)(2,1)S(1)}, bf16[1,128,2048]{2,1,0:T(8,128)(2,1)S(1)}, bf16[1,128,512]{2,1,0:T(8,128)(2,1)S(1)}, bf16[1,128,512...) custom-call(bf16[1,128,2048]{2,1,0:T(8,128)(2,1)} %q_hbm.1, bf16[1,128,512]{2,1,0:T(8,128)(2,1)} %rk_hbm.1, ...), custom_call_target="tpu_custom_call" | custom-call | tf_op jit(solution)/shard_map/pallas_call | solution.py:292
  37.5 1.1 %shard_map.128 = (bf16[1,128,2048]{2,1,0:T(8,128)(2,1)}, bf16[1,128,2048]{2,1,0:T(8,128)(2,1)}, bf16[1,128,512]{2,1,0:T(8,128)(2,1)}, bf16[1,128,512]{2,1,0:T(8,...) custom-call(bf16[1,128,2048]{2,1,0:T(8,128)(2,1)S(1)} %get-tuple-element.12.refs_0_, ...), custom_call_target="tpu_custom_call" | custom-call | tf_op jit(solution)/shard_map/pallas_call | solution.py:331

commit v3 on v2

--- a/solution.py
+++ b/solution.py
@@ -243,6 +243,8 @@
             pass_core(2)
         if h >= 1:
             add_pair(h - 1)
+        if h == last:
+            add_core(h)
 
     for h in range(KV_HEADS):
         gather_core(h, 1 - c).wait_recv()
@@ -251,7 +253,8 @@
             pass_pair(3)
         if h == 1:
             pass_core(3)
-        add_core(h)
+        if h < last:
+            add_core(h)
     add_far(0)
     add_pair(last)
     for h in range(1, last):

time: 38.8 us -> 38.6 us (level)
  no operation moved by 1% of the time
where the time goes in v3:
time: 38.6 us; the launch traced here: 38.4 us
  Pallas kernels  36.5 us (95%)
  between operations  1.93 us (5%)
    pallas_call x1, Pallas kernels, on_device(): pl.pallas_call(functools.partial(kernel, far), out_shape=(pltpu.VMEM(quer...  35.3 us
    pallas_call x1, Pallas kernels, on_device(): pl.pallas_call(store_kernel, out_shape=tuple((jax.ShapeDtypeStruct(x.shap...  1.14 us

profile of v3, /device:TPU:0, one launch (start us, length us, event | category | flops | bytes accessed | tf_op | source)
XLA Modules:
  0.0 38.4 jit_solution(12620137755388402510)
XLA Ops:
  1.9 35.3 %shard_map.127 = (bf16[1,128,2048]{2,1,0:T(8,128)(2,1)S(1)}, bf16[1,128,2048]{2,1,0:T(8,128)(2,1)S(1)}, bf16[1,128,512]{2,1,0:T(8,128)(2,1)S(1)}, bf16[1,128,512...) custom-call(bf16[1,128,2048]{2,1,0:T(8,128)(2,1)} %q_hbm.1, bf16[1,128,512]{2,1,0:T(8,128)(2,1)} %rk_hbm.1, ...), custom_call_target="tpu_custom_call" | custom-call | tf_op jit(solution)/shard_map/pallas_call | solution.py:295
  37.3 1.1 %shard_map.128 = (bf16[1,128,2048]{2,1,0:T(8,128)(2,1)}, bf16[1,128,2048]{2,1,0:T(8,128)(2,1)}, bf16[1,128,512]{2,1,0:T(8,128)(2,1)}, bf16[1,128,512]{2,1,0:T(8,...) custom-call(bf16[1,128,2048]{2,1,0:T(8,128)(2,1)S(1)} %get-tuple-element.12.refs_0_, ...), custom_call_target="tpu_custom_call" | custom-call | tf_op jit(solution)/shard_map/pallas_call | solution.py:334
